TPU v7x, 32 devices: a whole 2x2x4 slice. The times are simulated.
32 devices in a mesh: slab: 16 (over z, y, x), batch: 2 (over core).
Axes of the slice: x: 2, y: 2, z: 4, core: 2. Of those that a mesh axis runs over, the one named last changes fastest.
Arguments:
- query_rows: bfloat16 [1792, 1536], P(('batch', 'slab')), parts along dimension 0, may hold values from -48 to 48
- key_rows: bfloat16 [1792, 1536], P(('batch', 'slab')), parts along dimension 0, may hold values from -6 to 6
- value_rows: bfloat16 [1792, 1536], P(('batch', 'slab')), parts along dimension 0, may hold values from -6 to 6
Outputs:
- attended: bfloat16 [1792, 1536], P(('batch', 'slab')), parts along dimension 0
There are 2 independent parts, one for each index of `batch`. A program takes and returns all parts, laid end to end along the dimension named above; each array names one. Nothing has to cross between parts.
All inputs are finite; a program needn't handle non-finite values.
Results may differ from a plain program's by a relative error of at most 0.005.
Values may be sent and summed in bfloat16 or wider, within the bound.
No kernel may reach another device: no remote copies, remote signals or barrier semaphores. Data moves between devices by JAX's collectives and lax.ppermute only.
A program may use at most 64 MiB of HBM per device.

v0:
```python
import jax
import jax.numpy as jnp
from jax import lax
from jax.sharding import PartitionSpec as P

HEAD_DIM = 64


def partner(shard, axis, bit):
    return lax.ppermute(shard, axis, [(i, i ^ 1 << bit) for i in range(lax.axis_size(axis))])


def shifted(block, axis, distance):
    devices = range(lax.axis_size(axis))
    route = [((i - distance) % len(devices), i) for i in devices]
    return lax.ppermute(block, axis, route)


def regroup(slots, rank, mover):
    for bit in (0, 1):
        axis = 1 - bit
        mine = rank >> bit & 1
        keep = lax.dynamic_index_in_dim(slots, mine, axis, keepdims=False)
        send = lax.dynamic_index_in_dim(slots, 1 - mine, axis, keepdims=False)
        got = mover(send, bit)
        slots = jnp.where(mine == 0, jnp.stack([keep, got], axis), jnp.stack([got, keep], axis))
    return slots


def move_heads(piece, bit):
    return partner(piece, "slab", bit)


def move_tokens(piece, bit):
    return partner(piece, "slab", bit)


def on_device(query_rows, key_rows, value_rows):
    count = query_rows.shape[0]
    width = query_rows.shape[1]
    heads = width // HEAD_DIM
    group_heads = heads // 4
    part_width = width // 4
    scale = HEAD_DIM ** (-0.5)
    rank = lax.axis_index("slab")
    stacked = jnp.stack([query_rows, key_rows, value_rows], 0).reshape(3, count, 4, part_width)
    slots = jnp.transpose(stacked, (2, 0, 1, 3)).reshape(2, 2, 3, count, part_width)
    slots = regroup(slots, rank, move_heads)
    local = jnp.transpose(slots.reshape(4, 3, count, part_width), (1, 0, 2, 3)).reshape(
        3, 4 * count, part_width
    )
    rows = 4 * count
    queries = local[0].reshape(rows, group_heads, HEAD_DIM)
    own_block = local[1:3]

    def absorb(carry, block):
        run_max, run_total, accum = carry
        key_block = block[0].reshape(-1, group_heads, HEAD_DIM)
        value_block = block[1].reshape(-1, group_heads, HEAD_DIM)
        scores = (
            jnp.einsum("qhd,khd->qhk", queries, key_block, preferred_element_type=jnp.float32)
            * scale
        )
        new_max = jnp.maximum(run_max, jnp.max(scores, axis=-1))
        shrink = jnp.exp(run_max - new_max)
        expo = jnp.exp(scores - new_max[..., None])
        new_total = run_total * shrink + jnp.sum(expo, axis=-1)
        mixed = jnp.einsum(
            "qhk,khd->qhd",
            expo.astype(jnp.bfloat16),
            value_block,
            preferred_element_type=jnp.float32,
        )
        return (new_max, new_total, accum * shrink[..., None] + mixed)

    start_state = (
        jnp.full((rows, group_heads), -1e30, jnp.float32),
        jnp.zeros((rows, group_heads), jnp.float32),
        jnp.zeros((rows, group_heads, HEAD_DIM), jnp.float32),
    )
    state = absorb(start_state, own_block)
    groups = lax.axis_size("slab") // 4

    def one_way(step, pack):
        carry, moving = pack
        moving = shifted(moving, "slab", 4)
        return (absorb(carry, moving), moving)

    state, moving = lax.fori_loop(0, groups - 1, one_way, (state, own_block))
    result = (state[2] / state[1][..., None]).astype(jnp.bfloat16)
    back_slots = result.reshape(2, 2, count, part_width)
    back_slots = regroup(back_slots, rank, move_tokens)
    return jnp.transpose(back_slots.reshape(4, count, part_width), (1, 0, 2)).reshape(count, width)


def solution(mesh):
    return jax.shard_map(
        on_device,
        mesh=mesh,
        in_specs=(
            P(("batch", "slab"), None),
            P(("batch", "slab"), None),
            P(("batch", "slab"), None),
        ),
        out_specs=P(("batch", "slab"), None),
        check_vma=False,
    )
```

profile of v0, /device:TPU:0, one launch (start us, length us, event | category | flops | bytes accessed | tf_op | source)
XLA Modules:
  0.0 69.0 jit_solution(4820081369436153990)
XLA Ops:
  0.0 1.0 %stack.60 = bf16[1,56,4,384]{3,2,1,0:T(4,128)(2,1)S(1)} reshape(bf16[56,1536]{1,0:T(8,128)(2,1)} %param.5) | data formatting | bytes 344064 | tf_op jit(solution)/shard_map/stack | solution.py:46
  1.0 1.0 %stack.61 = bf16[1,56,4,384]{3,2,1,0:T(4,128)(2,1)S(1)} reshape(bf16[56,1536]{1,0:T(8,128)(2,1)} %param.6) | data formatting | bytes 344064 | tf_op jit(solution)/shard_map/stack | solution.py:46
  1.9 1.0 %stack.62 = bf16[1,56,4,384]{3,2,1,0:T(4,128)(2,1)S(1)} reshape(bf16[56,1536]{1,0:T(8,128)(2,1)} %param.7) | data formatting | bytes 344064 | tf_op jit(solution)/shard_map/stack | solution.py:46
  2.9 0.4 maximum_bitcast_fusion
  3.5 3.0 %collective-permute-start.1 = (bf16[2,3,56,384]{3,2,1,0:T(8,128)(2,1)S(1)}, bf16[2,3,56,384]{3,2,1,0:T(8,128)(2,1)S(1)}, u32[]{:S(2)}, u32[]{:S(2)}) collective-permute-start(bf16[2,3,56,384]{3,2,1,0:T(8,128)(2,1)S(1)} %get-tuple-element.88), channel_id=1, source_target_pairs={{0,2},{2,0},{4,6},{6,4},{8,10},{10,8},{12,14},{14,12},{16,18},{18,... | collective-permute-start | bytes 774152 | tf_op jit(solution)/shard_map/ppermute | solution.py:10
  6.5 6.2 %collective-permute-done.1 = bf16[2,3,56,384]{3,2,1,0:T(8,128)(2,1)S(1)} collective-permute-done((bf16[2,3,56,384]{3,2,1,0:T(8,128)(2,1)S(1)}, bf16[2,3,56,384]{3,2,1,0:T(8,128)(2,1)S(1)}, u32[]{:S(2)}, u32[]{:S(2)}) %collective-permute-start.1) | collective-permute-done | bytes 258080 | tf_op jit(solution)/shard_map/ppermute | solution.py:10
  12.9 1.8 %collective-permute-start.2 = (bf16[2,3,56,384]{3,2,1,0:T(8,128)(2,1)S(1)}, bf16[2,3,56,384]{3,2,1,0:T(8,128)(2,1)S(1)}, u32[]{:S(2)}, u32[]{:S(2)}) collective-permute-start(bf16[2,3,56,384]{3,2,1,0:T(8,128)(2,1)S(1)} %get-tuple-element.86), channel_id=1, source_target_pairs={{0,4},{2,6},{4,0},{6,2},{8,12},{10,14},{12,8},{14,10},{16,20},{18,... | collective-permute-start | bytes 774152 | tf_op jit(solution)/shard_map/ppermute | solution.py:10
  14.8 5.6 %collective-permute-done.2 = bf16[2,3,56,384]{3,2,1,0:T(8,128)(2,1)S(1)} collective-permute-done((bf16[2,3,56,384]{3,2,1,0:T(8,128)(2,1)S(1)}, bf16[2,3,56,384]{3,2,1,0:T(8,128)(2,1)S(1)}, u32[]{:S(2)}, u32[]{:S(2)}) %collective-permute-start.2) | collective-permute-done | bytes 258080 | tf_op jit(solution)/shard_map/ppermute | solution.py:10
  20.8 0.3 reshape.49
  21.1 0.3 reshape.48
  21.6 0.3 reshape.47
  21.9 0.3 fusion.18
  22.5 0.3 fusion.9
  22.8 34.6 %while.16 = (s32[]{:T(128)}, f32[224,6]{0,1:T(8,128)S(1)}, f32[224,6]{0,1:T(8,128)S(1)}, f32[224,6,64]{0,2,1:T(8,128)S(1)}, bf16[2,224,384]{1,2,0:T(8,128)(2,1)S(1)}, /*index=5*/bf16[224,6,64]{0,2,1:T(8,128)(2,1)S(1)}, s32[]{:T(128)}) while((s32[]{:T(128)}, f32[224,6]{0,1:T(8,128)S(1)}, f32[224,6]{0,1:T(8,128)S(1)}, ...), condition=%wide.region_5.6_spmd, body=%wide.region_2.5_spmd.sunk | while | flops 79051392 | bytes 7655541 | solution.py:89
  22.9 1.6 %collective-permute-start = (bf16[2,224,384]{1,2,0:T(8,128)(2,1)S(1)}, bf16[2,224,384]{1,2,0:T(8,128)(2,1)S(1)}, u32[]{:S(2)}, u32[]{:S(2)}) collective-permute-start(bf16[2,224,384]{1,2,0:T(8,128)(2,1)S(1)} %get-tuple-element.157), channel_id=1, source_target_pairs={{24,0},{26,2},{28,4},{30,6},{0,8},{2,10},{4,12},{6,14},{8,16},{10,... | collective-permute-start | bytes 1032200 | tf_op jit(solution)/shard_map/while/body/eval_jaxpr/ppermute | solution.py:16
  24.4 9.7 %collective-permute-done = bf16[2,224,384]{1,2,0:T(8,128)(2,1)S(1)} collective-permute-done((bf16[2,224,384]{1,2,0:T(8,128)(2,1)S(1)}, bf16[2,224,384]{1,2,0:T(8,128)(2,1)S(1)}, u32[]{:S(2)}, u32[]{:S(2)}) %collective-permute-start) | collective-permute-done | bytes 344096 | tf_op jit(solution)/shard_map/while/body/eval_jaxpr/ppermute | solution.py:16
  34.1 0.4 fusion.36
  34.8 0.4 fusion.38
  35.3 10.2 %collective-permute-done = bf16[2,224,384]{1,2,0:T(8,128)(2,1)S(1)} collective-permute-done((bf16[2,224,384]{1,2,0:T(8,128)(2,1)S(1)}, bf16[2,224,384]{1,2,0:T(8,128)(2,1)S(1)}, u32[]{:S(2)}, u32[]{:S(2)}) %collective-permute-start) | collective-permute-done | bytes 344096 | tf_op jit(solution)/shard_map/while/body/eval_jaxpr/ppermute | solution.py:16
  45.6 0.4 fusion.36
  46.2 0.4 fusion.38
  46.7 9.6 %collective-permute-done = bf16[2,224,384]{1,2,0:T(8,128)(2,1)S(1)} collective-permute-done((bf16[2,224,384]{1,2,0:T(8,128)(2,1)S(1)}, bf16[2,224,384]{1,2,0:T(8,128)(2,1)S(1)}, u32[]{:S(2)}, u32[]{:S(2)}) %collective-permute-start) | collective-permute-done | bytes 344096 | tf_op jit(solution)/shard_map/while/body/eval_jaxpr/ppermute | solution.py:16
  56.3 0.4 fusion.36
  57.0 0.4 fusion.38
  57.7 0.8 %constant_dynamic-slice_fusion.2 = (bf16[2,1,56,384]{2,1,0,3:T(2,128)(2,1)S(1)}, bf16[2,1,56,384]{2,1,0,3:T(2,128)(2,1)S(1)}) fusion(bf16[2,2,56,384]{2,1,0,3:T(2,128)(2,1)S(1)} %reshape.45, s32[]{:T(128)S(6)} %select_n.60, s32[]{:T(128)S(6)} %select_n.61), kind=kLoop, calls=%fused_computation.33 | loop fusion | bytes 344072 | tf_op jit(solution)/shard_map/jit(dynamic_index_in_dim)/dynamic_slice | solution.py:23
  58.5 0.5 copy.56
  59.1 1.0 %collective-permute-start.3 = (bf16[2,56,384]{2,1,0:T(8,128)(2,1)S(1)}, bf16[2,56,384]{2,1,0:T(8,128)(2,1)S(1)}, u32[]{:S(2)}, u32[]{:S(2)}) collective-permute-start(bf16[2,56,384]{2,1,0:T(8,128)(2,1)S(1)} %bitcast.84), channel_id=1, source_target_pairs={{0,2},{2,0},{4,6},{6,4},{8,10},{10,8},{12,14},{14,12},{16,18},{18,... | collective-permute-start | bytes 258056 | tf_op jit(solution)/shard_map/ppermute | solution.py:10
  60.0 0.5 copy.57
  60.6 3.1 %collective-permute-done.3 = bf16[2,56,384]{2,1,0:T(8,128)(2,1)S(1)} collective-permute-done((bf16[2,56,384]{2,1,0:T(8,128)(2,1)S(1)}, bf16[2,56,384]{2,1,0:T(8,128)(2,1)S(1)}, u32[]{:S(2)}, u32[]{:S(2)}) %collective-permute-start.3) | collective-permute-done | bytes 86048 | tf_op jit(solution)/shard_map/ppermute | solution.py:10
  63.7 1.0 %collective-permute-start.4 = (bf16[2,56,384]{2,1,0:T(8,128)(2,1)S(1)}, bf16[2,56,384]{2,1,0:T(8,128)(2,1)S(1)}, u32[]{:S(2)}, u32[]{:S(2)}) collective-permute-start(bf16[2,56,384]{2,1,0:T(8,128)(2,1)S(1)} %get-tuple-element.92), channel_id=1, source_target_pairs={{0,4},{2,6},{4,0},{6,2},{8,12},{10,14},{12,8},{14,10},{16,20},{18,... | collective-permute-start | bytes 258056 | tf_op jit(solution)/shard_map/ppermute | solution.py:10
  64.7 3.6 %collective-permute-done.4 = bf16[2,56,384]{2,1,0:T(8,128)(2,1)S(1)} collective-permute-done((bf16[2,56,384]{2,1,0:T(8,128)(2,1)S(1)}, bf16[2,56,384]{2,1,0:T(8,128)(2,1)S(1)}, u32[]{:S(2)}, u32[]{:S(2)}) %collective-permute-start.4) | collective-permute-done | bytes 86048 | tf_op jit(solution)/shard_map/ppermute | solution.py:10
  68.3 0.7 copy.67
  (38 shorter events, 2.6 us)
Async XLA Ops:
  3.5 9.2 %collective-permute-start.1 = (bf16[2,3,56,384]{3,2,1,0:T(8,128)(2,1)S(1)}, bf16[2,3,56,384]{3,2,1,0:T(8,128)(2,1)S(1)}, u32[]{:S(2)}, u32[]{:S(2)}) collective-permute-start(bf16[2,3,56,384]{3,2,1,0:T(8,128)(2,1)S(1)} %get-tuple-element.88), channel_id=1, source_target_pairs={{0,2},{2,0},{4,6},{6,4},{8,10},{10,8},{12,14},{14,12},{16,18},{18,... | collective-permute-start | bytes 774152 | tf_op jit(solution)/shard_map/ppermute | solution.py:10
  12.9 7.5 %collective-permute-start.2 = (bf16[2,3,56,384]{3,2,1,0:T(8,128)(2,1)S(1)}, bf16[2,3,56,384]{3,2,1,0:T(8,128)(2,1)S(1)}, u32[]{:S(2)}, u32[]{:S(2)}) collective-permute-start(bf16[2,3,56,384]{3,2,1,0:T(8,128)(2,1)S(1)} %get-tuple-element.86), channel_id=1, source_target_pairs={{0,4},{2,6},{4,0},{6,2},{8,12},{10,14},{12,8},{14,10},{16,20},{18,... | collective-permute-start | bytes 774152 | tf_op jit(solution)/shard_map/ppermute | solution.py:10
  22.9 11.2 %collective-permute-start = (bf16[2,224,384]{1,2,0:T(8,128)(2,1)S(1)}, bf16[2,224,384]{1,2,0:T(8,128)(2,1)S(1)}, u32[]{:S(2)}, u32[]{:S(2)}) collective-permute-start(bf16[2,224,384]{1,2,0:T(8,128)(2,1)S(1)} %get-tuple-element.157), channel_id=1, source_target_pairs={{24,0},{26,2},{28,4},{30,6},{0,8},{2,10},{4,12},{6,14},{8,16},{10,... | collective-permute-start | bytes 1032200 | tf_op jit(solution)/shard_map/while/body/eval_jaxpr/ppermute | solution.py:16
  35.2 10.3 %collective-permute-start = (bf16[2,224,384]{1,2,0:T(8,128)(2,1)S(1)}, bf16[2,224,384]{1,2,0:T(8,128)(2,1)S(1)}, u32[]{:S(2)}, u32[]{:S(2)}) collective-permute-start(bf16[2,224,384]{1,2,0:T(8,128)(2,1)S(1)} %get-tuple-element.157), channel_id=1, source_target_pairs={{24,0},{26,2},{28,4},{30,6},{0,8},{2,10},{4,12},{6,14},{8,16},{10,... | collective-permute-start | bytes 1032200 | tf_op jit(solution)/shard_map/while/body/eval_jaxpr/ppermute | solution.py:16
  46.7 9.6 %collective-permute-start = (bf16[2,224,384]{1,2,0:T(8,128)(2,1)S(1)}, bf16[2,224,384]{1,2,0:T(8,128)(2,1)S(1)}, u32[]{:S(2)}, u32[]{:S(2)}) collective-permute-start(bf16[2,224,384]{1,2,0:T(8,128)(2,1)S(1)} %get-tuple-element.157), channel_id=1, source_target_pairs={{24,0},{26,2},{28,4},{30,6},{0,8},{2,10},{4,12},{6,14},{8,16},{10,... | collective-permute-start | bytes 1032200 | tf_op jit(solution)/shard_map/while/body/eval_jaxpr/ppermute | solution.py:16
  59.1 4.6 %collective-permute-start.3 = (bf16[2,56,384]{2,1,0:T(8,128)(2,1)S(1)}, bf16[2,56,384]{2,1,0:T(8,128)(2,1)S(1)}, u32[]{:S(2)}, u32[]{:S(2)}) collective-permute-start(bf16[2,56,384]{2,1,0:T(8,128)(2,1)S(1)} %bitcast.84), channel_id=1, source_target_pairs={{0,2},{2,0},{4,6},{6,4},{8,10},{10,8},{12,14},{14,12},{16,18},{18,... | collective-permute-start | bytes 258056 | tf_op jit(solution)/shard_map/ppermute | solution.py:10
  63.7 4.6 %collective-permute-start.4 = (bf16[2,56,384]{2,1,0:T(8,128)(2,1)S(1)}, bf16[2,56,384]{2,1,0:T(8,128)(2,1)S(1)}, u32[]{:S(2)}, u32[]{:S(2)}) collective-permute-start(bf16[2,56,384]{2,1,0:T(8,128)(2,1)S(1)} %get-tuple-element.92), channel_id=1, source_target_pairs={{0,4},{2,6},{4,0},{6,2},{8,12},{10,14},{12,8},{14,10},{16,20},{18,... | collective-permute-start | bytes 258056 | tf_op jit(solution)/shard_map/ppermute | solution.py:10
where the time goes:
time: 69.2 us; the launch traced here: 69 us
  waiting for transfers between devices  47.9 us (69%)
  starting transfers between devices  8.47 us (12%)
  local copies, waits for them, and re-layouts  7.43 us (11%)
  matrix products  2.99 us (4%)
  other arithmetic  1.72 us (2%)
    ppermute x3, waiting for transfers between devices, shifted(): return lax.ppermute(block, axis, route)  29.5 us
    ppermute x4, waiting for transfers between devices, partner(): lax.ppermute(shard, axis, [(i, i ^ 1 << bit) for i in range(lax.axis_size...  18.5 us
    ppermute x4, starting transfers between devices, partner(): lax.ppermute(shard, axis, [(i, i ^ 1 << bit) for i in range(lax.axis_size...  6.78 us
    another operation x3, local copies, waits for them, and re-layouts, on_device(): jnp.stack([query_rows, key_rows, value_rows], 0)  2.89 us
    ppermute x3, starting transfers between devices, shifted(): return lax.ppermute(block, axis, route)  1.68 us
    dot_general x4, matrix products, absorb(): jnp.einsum('qhd,khd->qhk', queries, key_block, preferred_element_type=jnp...  1.53 us
    dynamic_slice x5, local copies, waits for them, and re-layouts, regroup(): keep = lax.dynamic_index_in_dim(slots, mine, axis, keepdims=False)  1.52 us
    dot_general x4, matrix products, absorb(): jnp.einsum('qhk,khd->qhd', expo.astype(jnp.bfloat16), value_block, prefer...  1.46 us
  transfers between devices with their start and end apart: 7, of which 7 were waited for; matrix products, arithmetic and copies ran while one was open for 1% of the time, Pallas kernels for 0%

commit v1 on v0

v1 whole, which is shorter than its diff:
```python
import jax
import jax.numpy as jnp
from jax import lax
from jax.experimental import pallas as pl
from jax.experimental.pallas import tpu as pltpu
from jax.sharding import PartitionSpec as P

HEAD_DIM = 64
PAIR = 2 * HEAD_DIM
TRIPLE = 3 * HEAD_DIM
LOG2E = 1.4426950408889634


def window(owner):
    return (owner // 2) * TRIPLE + (owner % 2) * HEAD_DIM


def pack_kernel(owners, q_ref, k_ref, v_ref, out_ref):
    for owner in range(owners):
        start = window(owner)
        for place, ref in enumerate((k_ref, v_ref, q_ref)):
            out_ref[owner, place] = ref[:, start : start + PAIR]


def pack(owners, q, k, v):
    count = q.shape[0]
    return pl.pallas_call(
        lambda *refs: pack_kernel(owners, *refs),
        out_shape=jax.ShapeDtypeStruct((owners, 3, count, PAIR), q.dtype),
    )(q, k, v)


def attend_kernel(got_ref, out_ref, k_ref, va_ref, vc_ref):
    owners, _, count, _ = got_ref.shape
    first = lax.broadcasted_iota(jnp.int32, (count, PAIR), 1) < HEAD_DIM
    one = jnp.ones((count, PAIR), k_ref.dtype)
    zero = jnp.zeros((count, PAIR), k_ref.dtype)
    for s in range(owners):
        rows = pl.ds(s * count, count)
        k_ref[rows, :] = got_ref[s, 0]
        v = got_ref[s, 1]
        va_ref[rows, :] = jnp.where(first, v, one)
        vc_ref[rows, :] = jnp.where(first, one, v)
    keys = k_ref[...]
    factor = HEAD_DIM**-0.5 * LOG2E

    def mixed(queries, values):
        scores = lax.dot_general(
            queries, keys, (((1,), (1,)), ((), ())), preferred_element_type=jnp.float32
        )
        top = jnp.max(scores, axis=-1, keepdims=True)
        expo = jnp.exp2((scores - top) * factor).astype(keys.dtype)
        return jnp.dot(expo, values, preferred_element_type=jnp.float32)

    for s in range(owners):
        q = got_ref[s, 2]
        a = mixed(jnp.where(first, q, zero), va_ref[...])
        c = mixed(jnp.where(first, zero, q), vc_ref[...])
        total = pltpu.roll(jnp.where(first, c, a), HEAD_DIM, 1)
        out_ref[s] = (jnp.where(first, a, c) / total).astype(out_ref.dtype)


def attend(got):
    owners, _, count, _ = got.shape
    rows = owners * count
    return pl.pallas_call(
        attend_kernel,
        out_shape=jax.ShapeDtypeStruct((owners, count, PAIR), got.dtype),
        scratch_shapes=[pltpu.VMEM((rows, PAIR), got.dtype)] * 3,
        compiler_params=pltpu.CompilerParams(vmem_limit_bytes=32 * 1024 * 1024),
    )(got)


def unpack_kernel(back_ref, out_ref):
    owners, count, _ = back_ref.shape
    first = lax.broadcasted_iota(jnp.int32, (count, PAIR), 1) < HEAD_DIM
    for m in range(owners // 4):
        start = 3 * PAIR * m
        middle = jnp.where(first, back_ref[4 * m + 2], back_ref[4 * m + 1])
        out_ref[:, start : start + PAIR] = back_ref[4 * m]
        out_ref[:, start + PAIR : start + 2 * PAIR] = jnp.concatenate(
            [middle[:, HEAD_DIM:], middle[:, :HEAD_DIM]], axis=1
        )
        out_ref[:, start + 2 * PAIR : start + 3 * PAIR] = back_ref[4 * m + 3]


def unpack(back):
    owners, count, _ = back.shape
    return pl.pallas_call(
        unpack_kernel,
        out_shape=jax.ShapeDtypeStruct((count, owners // 4 * 3 * PAIR), back.dtype),
    )(back)


def attend_ring(got, owners):
    size = lax.axis_size("slab")
    _, _, count, _ = got.shape
    rows = owners * count
    tokens = jnp.transpose(got, (1, 0, 2, 3)).reshape(3, rows, 2, HEAD_DIM)
    queries = tokens[2]
    route = [(i, (i + owners) % size) for i in range(size)]

    def absorb(carry, block):
        run_max, run_total, accum = carry
        scores = jnp.einsum("qhd,khd->hqk", queries, block[0], preferred_element_type=jnp.float32)
        scores = scores * HEAD_DIM**-0.5
        new_max = jnp.maximum(run_max, jnp.max(scores, axis=-1))
        shrink = jnp.exp(run_max - new_max)
        expo = jnp.exp(scores - new_max[..., None])
        mix = jnp.einsum(
            "hqk,khd->hqd",
            expo.astype(jnp.bfloat16),
            block[1],
            preferred_element_type=jnp.float32,
        )
        total = run_total * shrink + jnp.sum(expo, axis=-1)
        return new_max, total, accum * shrink[..., None] + mix

    def step(_, pack):
        carry, moving = pack
        moving = lax.ppermute(moving, "slab", route)
        return absorb(carry, moving), moving

    state = (
        jnp.full((2, rows), -1e30, jnp.float32),
        jnp.zeros((2, rows), jnp.float32),
        jnp.zeros((2, rows, HEAD_DIM), jnp.float32),
    )
    state = absorb(state, tokens[:2])
    state, _ = lax.fori_loop(0, size // owners - 1, step, (state, tokens[:2]))
    result = (state[2] / state[1][..., None]).astype(got.dtype)
    return jnp.transpose(result, (1, 0, 2)).reshape(owners, count, PAIR)


def on_device(query_rows, key_rows, value_rows):
    size = lax.axis_size("slab")
    owners = query_rows.shape[1] // TRIPLE * 2
    groups = [list(range(g, g + owners)) for g in range(0, size, owners)]
    exchange = lambda x: lax.all_to_all(x, "slab", 0, 0, axis_index_groups=groups)
    got = exchange(pack(owners, query_rows, key_rows, value_rows))
    result = attend(got) if size == owners else attend_ring(got, owners)
    return unpack(exchange(result))


def solution(mesh):
    spec = P(("batch", "slab"), None)
    return jax.shard_map(
        on_device, mesh=mesh, in_specs=(spec,) * 3, out_specs=spec, check_vma=False
    )
```

time: 69.2 us -> 54.2 us (0.78)
  waiting for transfers between devices: 47.9 us -> 0 us
  blocking collectives: 0 us -> 39.3 us
  Pallas kernels: 0 us -> 14.6 us
  starting transfers between devices: 8.47 us -> 0 us
  local copies, waits for them, and re-layouts: 7.43 us -> 0 us
  matrix products: 2.99 us -> 0 us
  other arithmetic: 1.72 us -> 0 us
    ppermute x7 -> x0, waiting for transfers between devices: 47.9 us -> none  [the longest x3 29.5 us: shifted(): return lax.ppermute(block, axis, route)]
    all_to_all x0 -> x2, blocking collectives: none -> 39.3 us  [on_device(): lax.all_to_all(x, 'slab', 0, 0, axis_index_groups=groups)]
    pallas_call x0 -> x3, Pallas kernels: none -> 14.6 us  [the longest x1 10.7 us: attend(): pl.pallas_call(attend_kernel, out_shape=jax.ShapeDtypeStruct((owners, cou...]
    ppermute x7 -> x0, starting transfers between devices: 8.47 us -> none  [the longest x4 6.78 us: partner(): lax.ppermute(shard, axis, [(i, i ^ 1 << bit) for i in range(lax.axis_size...]
    another operation x7 -> x0, local copies, waits for them, and re-layouts: 3.92 us -> none  [the longest x3 2.89 us: on_device(): jnp.stack([query_rows, key_rows, value_rows], 0)]
    dot_general x8 -> x0, matrix products: 2.99 us -> none  [the longest x4 1.53 us: absorb(): jnp.einsum('qhd,khd->qhk', queries, key_block, preferred_element_type=jnp...]
    dynamic_slice x6 -> x0, local copies, waits for them, and re-layouts: 2.06 us -> none  [the longest x5 1.52 us: regroup(): keep = lax.dynamic_index_in_dim(slots, mine, axis, keepdims=False)]
    reshape x2 -> x0, local copies, waits for them, and re-layouts: 0.91 us -> none  [the longest x1 0.69 us: on_device(): jnp.transpose(back_slots.reshape(4, count, part_width), (1, 0, 2))]
  transfers between devices with their start and end apart: 7 -> 0, of which waited for: 7 -> 0; matrix products, arithmetic and copies ran while one was open for 1% -> 0% of each run, Pallas kernels for 0% -> 0%
where the time goes in v1:
time: 54.2 us; the launch traced here: 53.9 us
  blocking collectives  39.3 us (73%)
  Pallas kernels  14.6 us (27%)
    all_to_all x2, blocking collectives, on_device(): lax.all_to_all(x, 'slab', 0, 0, axis_index_groups=groups)  39.3 us
    pallas_call x1, Pallas kernels, attend(): pl.pallas_call(attend_kernel, out_shape=jax.ShapeDtypeStruct((owners, cou...  10.7 us
    pallas_call x1, Pallas kernels, pack(): pl.pallas_call(lambda *refs: pack_kernel(owners, *refs), out_shape=jax.Sh...  2.19 us
    pallas_call x1, Pallas kernels, unpack(): pl.pallas_call(unpack_kernel, out_shape=jax.ShapeDtypeStruct((count, owne...  1.7 us

profile of v1, /device:TPU:0, one launch (start us, length us, event | category | flops | bytes accessed | tf_op | source)
XLA Modules:
  0.0 53.9 jit_solution(9871463710609797081)
XLA Ops:
  0.0 2.2 %shard_map.37 = bf16[16,3,56,128]{3,2,1,0:T(8,128)(2,1)} custom-call(bf16[56,1536]{1,0:T(8,128)(2,1)} %refs_0_.1, bf16[56,1536]{1,0:T(8,128)(2,1)} %refs_1_.1, bf16[56,1536]{1,0:T(8,128)(2,1)} %refs_2_.1), custom_call_target="tpu_custom_call" | custom-call | tf_op jit(solution)/shard_map/pallas_call | solution.py:27
  2.2 27.7 %all_to_all.10.got_ref = bf16[16,3,56,128]{3,2,1,0:T(8,128)(2,1)S(1)} all-to-all(bf16[16,3,56,128]{3,2,1,0:T(8,128)(2,1)} %shard_map.37), channel_id=1, replica_groups={{0,2,4,6,8,10,12,14,16,18,20,22,24,26,28,30},{1,3,5,7,9,11,13,15,17,19,..., dimensions={0} | all-to-all | bytes 1376256 | tf_op jit(solution)/shard_map/all_to_all | solution.py:139
  29.9 10.7 %shard_map.38 = bf16[16,56,128]{2,1,0:T(8,128)(2,1)S(1)} custom-call(bf16[16,3,56,128]{3,2,1,0:T(8,128)(2,1)S(1)} %all_to_all.10.got_ref), custom_call_target="tpu_custom_call" | custom-call | tf_op jit(solution)/shard_map/pallas_call | solution.py:66
  40.6 11.6 %all_to_all.11.back_ref = bf16[16,56,128]{2,1,0:T(8,128)(2,1)} all-to-all(bf16[16,56,128]{2,1,0:T(8,128)(2,1)S(1)} %shard_map.38), channel_id=1, replica_groups={{0,2,4,6,8,10,12,14,16,18,20,22,24,26,28,30},{1,3,5,7,9,11,13,15,17,19,..., dimensions={0} | all-to-all | bytes 458752 | tf_op jit(solution)/shard_map/all_to_all | solution.py:139
  52.2 1.7 %shard_map.39 = bf16[56,1536]{1,0:T(8,128)(2,1)} custom-call(bf16[16,56,128]{2,1,0:T(8,128)(2,1)} %all_to_all.11.back_ref), custom_call_target="tpu_custom_call" | custom-call | tf_op jit(solution)/shard_map/pallas_call | solution.py:89

commit v2 on v1

--- a/solution.py
+++ b/solution.py
@@ -27,10 +27,11 @@
     return pl.pallas_call(
         lambda *refs: pack_kernel(owners, *refs),
         out_shape=jax.ShapeDtypeStruct((owners, 3, count, PAIR), q.dtype),
+        compiler_params=pltpu.CompilerParams(vmem_limit_bytes=8 * 1024 * 1024),
     )(q, k, v)
 
 
-def attend_kernel(got_ref, out_ref, k_ref, va_ref, vc_ref):
+def attend_kernel(got_ref, out_ref, k_ref, va_ref, vc_ref, qa_ref, qc_ref):
     owners, _, count, _ = got_ref.shape
     first = lax.broadcasted_iota(jnp.int32, (count, PAIR), 1) < HEAD_DIM
     one = jnp.ones((count, PAIR), k_ref.dtype)
@@ -41,23 +42,26 @@
         v = got_ref[s, 1]
         va_ref[rows, :] = jnp.where(first, v, one)
         vc_ref[rows, :] = jnp.where(first, one, v)
-    keys = k_ref[...]
+        q = got_ref[s, 2]
+        qa_ref[rows, :] = jnp.where(first, q, zero)
+        qc_ref[rows, :] = jnp.where(first, zero, q)
     factor = HEAD_DIM**-0.5 * LOG2E
 
-    def mixed(queries, values):
+    def mixed(q_ref, v_ref):
         scores = lax.dot_general(
-            queries, keys, (((1,), (1,)), ((), ())), preferred_element_type=jnp.float32
+            q_ref[...], k_ref[...], (((1,), (1,)), ((), ())), preferred_element_type=jnp.float32
         )
         top = jnp.max(scores, axis=-1, keepdims=True)
-        expo = jnp.exp2((scores - top) * factor).astype(keys.dtype)
-        return jnp.dot(expo, values, preferred_element_type=jnp.float32)
+        expo = jnp.exp2((scores - top) * factor).astype(k_ref.dtype)
+        return jnp.dot(expo, v_ref[...], preferred_element_type=jnp.float32)
 
+    a = mixed(qa_ref, va_ref)
+    c = mixed(qc_ref, vc_ref)
+    first = lax.broadcasted_iota(jnp.int32, a.shape, 1) < HEAD_DIM
+    total = pltpu.roll(jnp.where(first, c, a), HEAD_DIM, 1)
+    result = (jnp.where(first, a, c) / total).astype(out_ref.dtype)
     for s in range(owners):
-        q = got_ref[s, 2]
-        a = mixed(jnp.where(first, q, zero), va_ref[...])
-        c = mixed(jnp.where(first, zero, q), vc_ref[...])
-        total = pltpu.roll(jnp.where(first, c, a), HEAD_DIM, 1)
-        out_ref[s] = (jnp.where(first, a, c) / total).astype(out_ref.dtype)
+        out_ref[s] = result[s * count : (s + 1) * count]
 
 
 def attend(got):
@@ -66,7 +70,7 @@
     return pl.pallas_call(
         attend_kernel,
         out_shape=jax.ShapeDtypeStruct((owners, count, PAIR), got.dtype),
-        scratch_shapes=[pltpu.VMEM((rows, PAIR), got.dtype)] * 3,
+        scratch_shapes=[pltpu.VMEM((rows, PAIR), got.dtype)] * 5,
         compiler_params=pltpu.CompilerParams(vmem_limit_bytes=32 * 1024 * 1024),
     )(got)
 
@@ -89,6 +93,7 @@
     return pl.pallas_call(
         unpack_kernel,
         out_shape=jax.ShapeDtypeStruct((count, owners // 4 * 3 * PAIR), back.dtype),
+        compiler_params=pltpu.CompilerParams(vmem_limit_bytes=8 * 1024 * 1024),
     )(back)
 
 

time: 54.2 us -> 45.7 us (0.84)
  Pallas kernels: 14.6 us -> 3.87 us
  local copies, waits for them, and re-layouts: 0 us -> 2.75 us
    pallas_call x1, Pallas kernels: 10.7 us -> 2.86 us  [attend(): pl.pallas_call(attend_kernel, out_shape=jax.ShapeDtypeStruct((owners, cou...]
    unnamed x0 -> x6, local copies, waits for them, and re-layouts: none -> 2.75 us
    pallas_call x1, Pallas kernels: 2.19 us -> 0.26 us  [pack(): pl.pallas_call(lambda *refs: pack_kernel(owners, *refs), out_shape=jax.Sh...]
    pallas_call x1, Pallas kernels: 1.7 us -> 0.76 us  [unpack(): pl.pallas_call(unpack_kernel, out_shape=jax.ShapeDtypeStruct((count, owne...]
where the time goes in v2:
time: 45.7 us; the launch traced here: 45.4 us
  blocking collectives  38.8 us (85%)
  Pallas kernels  3.87 us (8%)
  local copies, waits for them, and re-layouts  2.75 us (6%)
    all_to_all x2, blocking collectives, on_device(): lax.all_to_all(x, 'slab', 0, 0, axis_index_groups=groups)  38.8 us
    pallas_call x1, Pallas kernels, attend(): pl.pallas_call(attend_kernel, out_shape=jax.ShapeDtypeStruct((owners, cou...  2.86 us
    unnamed x6, local copies, waits for them, and re-layouts  2.75 us

profile of v2, /device:TPU:0, one launch (start us, length us, event | category | flops | bytes accessed | tf_op | source)
XLA Modules:
  0.0 45.4 jit_solution(686209405247919474)
XLA Ops:
  0.0 0.0 copy-start
  0.0 0.9 %copy-done = bf16[56,1536]{1,0:T(8,128)(2,1)S(1)} copy-done((bf16[56,1536]{1,0:T(8,128)(2,1)S(1)}, bf16[56,1536]{1,0:T(8,128)(2,1)}, u32[]{:S(2)}) %copy-start) | copy-done | bytes 172056
  0.9 0.0 copy-start.1
  0.9 0.9 %copy-done.1 = bf16[56,1536]{1,0:T(8,128)(2,1)S(1)} copy-done((bf16[56,1536]{1,0:T(8,128)(2,1)S(1)}, bf16[56,1536]{1,0:T(8,128)(2,1)}, u32[]{:S(2)}) %copy-start.1) | copy-done | bytes 172056
  1.8 0.0 copy-start.2
  1.8 0.9 %copy-done.2 = bf16[56,1536]{1,0:T(8,128)(2,1)S(1)} copy-done((bf16[56,1536]{1,0:T(8,128)(2,1)S(1)}, bf16[56,1536]{1,0:T(8,128)(2,1)}, u32[]{:S(2)}) %copy-start.2) | copy-done | bytes 172056
  2.8 0.3 shard_map.37
  3.0 27.5 %all_to_all.10.got_ref = bf16[16,3,56,128]{3,2,1,0:T(8,128)(2,1)S(1)} all-to-all(bf16[16,3,56,128]{3,2,1,0:T(8,128)(2,1)S(1)} %shard_map.37), channel_id=1, replica_groups={{0,2,4,6,8,10,12,14,16,18,20,22,24,26,28,30},{1,3,5,7,9,11,13,15,17,19,..., dimensions={0} | all-to-all | bytes 1376256 | tf_op jit(solution)/shard_map/all_to_all | solution.py:144
  30.5 2.9 %shard_map.38 = bf16[16,56,128]{2,1,0:T(8,128)(2,1)S(1)} custom-call(bf16[16,3,56,128]{3,2,1,0:T(8,128)(2,1)S(1)} %all_to_all.10.got_ref), custom_call_target="tpu_custom_call" | custom-call | tf_op jit(solution)/shard_map/pallas_call | solution.py:70
  33.4 11.3 %all_to_all.11.back_ref = bf16[16,56,128]{2,1,0:T(8,128)(2,1)S(1)} all-to-all(bf16[16,56,128]{2,1,0:T(8,128)(2,1)S(1)} %shard_map.38), channel_id=1, replica_groups={{0,2,4,6,8,10,12,14,16,18,20,22,24,26,28,30},{1,3,5,7,9,11,13,15,17,19,..., dimensions={0} | all-to-all | bytes 458752 | tf_op jit(solution)/shard_map/all_to_all | solution.py:144
  44.7 0.8 %shard_map.39 = bf16[56,1536]{1,0:T(8,128)(2,1)} custom-call(bf16[16,56,128]{2,1,0:T(8,128)(2,1)S(1)} %all_to_all.11.back_ref), custom_call_target="tpu_custom_call" | custom-call | tf_op jit(solution)/shard_map/pallas_call | solution.py:93
Async XLA Ops:
  0.0 0.9 %copy-start = (bf16[56,1536]{1,0:T(8,128)(2,1)S(1)}, bf16[56,1536]{1,0:T(8,128)(2,1)}, u32[]{:S(2)}) copy-start(bf16[56,1536]{1,0:T(8,128)(2,1)} %refs_0_.1) | copy-start | bytes 516100
  0.9 0.9 %copy-start.1 = (bf16[56,1536]{1,0:T(8,128)(2,1)S(1)}, bf16[56,1536]{1,0:T(8,128)(2,1)}, u32[]{:S(2)}) copy-start(bf16[56,1536]{1,0:T(8,128)(2,1)} %refs_1_.1) | copy-start | bytes 516100
  1.8 0.9 %copy-start.2 = (bf16[56,1536]{1,0:T(8,128)(2,1)S(1)}, bf16[56,1536]{1,0:T(8,128)(2,1)}, u32[]{:S(2)}) copy-start(bf16[56,1536]{1,0:T(8,128)(2,1)} %refs_2_.1) | copy-start | bytes 516100

commit v3 on v2

v3 whole, which is shorter than its diff:
```python
import jax
import jax.numpy as jnp
from jax import lax
from jax.experimental import pallas as pl
from jax.experimental.pallas import tpu as pltpu
from jax.sharding import PartitionSpec as P

HEAD_DIM = 64
PAIR = 2 * HEAD_DIM
TRIPLE = 3 * HEAD_DIM
LOG2E = 1.4426950408889634
ROWS = 8


def folds(count):
    part = pl.cdiv(count, 2 * ROWS) * ROWS
    return part, pl.cdiv(count + part, 2 * ROWS) * ROWS


def lanes(shape):
    return lax.broadcasted_iota(jnp.int32, shape, 1) < HEAD_DIM


def swap(x):
    return jnp.concatenate([x[:, HEAD_DIM:], x[:, :HEAD_DIM]], axis=1)


def fold(whole, shared):
    count, part = whole.shape[0], shared.shape[0]
    rows = folds(count)[1]
    rest = [shared, swap(whole[rows:])]
    if part + count - rows < rows:
        rest.append(jnp.zeros((2 * rows - part - count, PAIR), whole.dtype))
    return jnp.where(lanes((rows, PAIR)), whole[:rows], jnp.concatenate(rest, axis=0))


def unfold(block, count):
    part, rows = folds(count)
    return jnp.concatenate([block, swap(block[part : part + count - rows])], axis=0), block[:part]


def pack_kernel(owners, q_hbm, k_hbm, v_hbm, out_ref, q_ref, k_ref, v_ref, sems):
    count = q_ref.shape[0]
    part, rows = folds(count)
    copies = [
        pltpu.make_async_copy(hbm, ref, sems.at[i])
        for i, (hbm, ref) in enumerate(((k_hbm, k_ref), (v_hbm, v_ref), (q_hbm, q_ref)))
    ]
    for copy in copies:
        copy.start()
    first = lanes((count, PAIR))

    def blocks(ref, m):
        left, middle, right = (ref[:, (3 * m + i) * PAIR : (3 * m + i + 1) * PAIR] for i in range(3))
        return left, jnp.where(first, middle, left), swap(jnp.where(first, right, middle)), swap(right)

    for place, (copy, ref) in enumerate(zip(copies, (k_ref, v_ref, q_ref))):
        copy.wait()
        for m in range(owners // 4):
            for i, block in enumerate(blocks(ref, m)):
                if place < 2:
                    out_ref[4 * m + i, place * count : (place + 1) * count] = block
                else:
                    shared = block[:part] if i % 2 == 0 else block[count - part :]
                    out_ref[4 * m + i, 2 * count :] = fold(block, shared)


def pack(owners, q, k, v):
    count = q.shape[0]
    return pl.pallas_call(
        lambda *refs: pack_kernel(owners, *refs),
        out_shape=jax.ShapeDtypeStruct((owners, 2 * count + folds(count)[1], PAIR), q.dtype),
        in_specs=[pl.BlockSpec(memory_space=pltpu.HBM)] * 3,
        scratch_shapes=[pltpu.VMEM(q.shape, q.dtype)] * 3 + [pltpu.SemaphoreType.DMA((3,))],
        compiler_params=pltpu.CompilerParams(vmem_limit_bytes=8 * 1024 * 1024),
    )(q, k, v)


def attend_kernel(count, got_ref, out_ref, k_ref, va_ref, vc_ref, qa_ref, qc_ref):
    owners = got_ref.shape[0]
    part, _ = folds(count)
    first = lanes((count, PAIR))
    one = jnp.ones((count, PAIR), k_ref.dtype)
    zero = jnp.zeros((count, PAIR), k_ref.dtype)
    for s in range(owners):
        rows = pl.ds(s * count, count)
        k_ref[rows, :] = got_ref[s, :count]
        v = got_ref[s, count : 2 * count]
        va_ref[rows, :] = jnp.where(first, v, one)
        vc_ref[rows, :] = jnp.where(first, one, v)
        whole, shared = unfold(got_ref[s, 2 * count :], count)
        qa_ref[rows, :] = jnp.where(first, whole, zero)
        qc_ref[pl.ds(s * part, part), :] = jnp.where(first[:part], zero[:part], shared)
    factor = HEAD_DIM**-0.5 * LOG2E

    def attended(q_ref, v_ref):
        scores = lax.dot_general(
            q_ref[...], k_ref[...], (((1,), (1,)), ((), ())), preferred_element_type=jnp.float32
        )
        top = jnp.max(scores, axis=-1, keepdims=True)
        expo = jnp.exp2((scores - top) * factor).astype(k_ref.dtype)
        mixed = jnp.dot(expo, v_ref[...], preferred_element_type=jnp.float32)
        return (mixed / pltpu.roll(mixed, HEAD_DIM, 1)).astype(out_ref.dtype)

    a = attended(qa_ref, va_ref)
    c = attended(qc_ref, vc_ref)
    for s in range(owners):
        out_ref[s] = fold(a[s * count : (s + 1) * count], c[s * part : (s + 1) * part])


def attend(got, count):
    owners = got.shape[0]
    part, rows = folds(count)
    whole, shared = pltpu.VMEM((owners * count, PAIR), got.dtype), pltpu.VMEM((owners * part, PAIR), got.dtype)
    return pl.pallas_call(
        lambda *refs: attend_kernel(count, *refs),
        out_shape=jax.ShapeDtypeStruct((owners, rows, PAIR), got.dtype),
        scratch_shapes=[whole] * 4 + [shared],
        compiler_params=pltpu.CompilerParams(vmem_limit_bytes=32 * 1024 * 1024),
    )(got)


def unpack_kernel(count, back_ref, out_ref):
    part, _ = folds(count)
    first = lanes((count, PAIR))
    for m in range(back_ref.shape[0] // 4):
        (a, ca), (b, cb), (d, cd), (e, ce) = (
            unfold(back_ref[4 * m + i], count) for i in range(4)
        )
        repeated = 2 * part - count
        tiles = (
            jnp.where(first, a, jnp.concatenate([ca, cb[repeated:]], axis=0)),
            jnp.where(first, b, swap(d)),
            swap(jnp.where(first, e, jnp.concatenate([cd, ce[repeated:]], axis=0))),
        )
        for i, tile in enumerate(tiles):
            out_ref[:, (3 * m + i) * PAIR : (3 * m + i + 1) * PAIR] = tile


def unpack(back, count):
    owners = back.shape[0]
    return pl.pallas_call(
        lambda *refs: unpack_kernel(count, *refs),
        out_shape=jax.ShapeDtypeStruct((count, owners // 4 * 3 * PAIR), back.dtype),
        compiler_params=pltpu.CompilerParams(vmem_limit_bytes=8 * 1024 * 1024),
    )(back)


def attend_ring(got, count):
    owners = got.shape[0]
    size = lax.axis_size("slab")
    part, rows = folds(count)
    split = lambda x: x.reshape(-1, 2, HEAD_DIM)
    own = jnp.stack([split(got[:, :count]), split(got[:, count : 2 * count])])
    whole, shared = jax.vmap(lambda block: unfold(block, count))(got[:, 2 * count :])
    queries = split(whole)[:, 0], split(shared)[:, 1]
    route = [(i, (i + owners) % size) for i in range(size)]

    def absorb(state, block):
        after = []
        for head, (q, (run_max, run_total, accum)) in enumerate(zip(queries, state)):
            scores = jnp.dot(q, block[0, :, head].T, preferred_element_type=jnp.float32) * HEAD_DIM**-0.5
            new_max = jnp.maximum(run_max, jnp.max(scores, axis=-1, keepdims=True))
            shrink = jnp.exp(run_max - new_max)
            expo = jnp.exp(scores - new_max)
            total = run_total * shrink + jnp.sum(expo, axis=-1, keepdims=True)
            mixed = jnp.dot(
                expo.astype(block.dtype), block[1, :, head], preferred_element_type=jnp.float32
            )
            after.append((new_max, total, accum * shrink + mixed))
        return tuple(after)

    def step(_, carry):
        state, moving = carry
        moving = lax.ppermute(moving, "slab", route)
        return absorb(state, moving), moving

    state = tuple(
        (
            jnp.full((q.shape[0], 1), -1e30, jnp.float32),
            jnp.zeros((q.shape[0], 1), jnp.float32),
            jnp.zeros(q.shape, jnp.float32),
        )
        for q in queries
    )
    state, _ = lax.fori_loop(0, size // owners - 1, step, (absorb(state, own), own))
    a, c = ((accum / total).astype(got.dtype) for _, total, accum in state)
    a, c = jnp.pad(a, ((0, 0), (0, HEAD_DIM))), jnp.pad(c, ((0, 0), (HEAD_DIM, 0)))
    return jax.vmap(fold)(a.reshape(owners, count, PAIR), c.reshape(owners, part, PAIR))


def on_device(query_rows, key_rows, value_rows):
    size = lax.axis_size("slab")
    count = query_rows.shape[0]
    owners = query_rows.shape[1] // TRIPLE * 2
    groups = [[g + i for i in members(owners)] for g in range(0, size, owners)]

    def exchange(blocks):
        return lax.all_to_all(blocks, "slab", 0, 0, axis_index_groups=groups)

    got = exchange(pack(owners, query_rows, key_rows, value_rows))
    result = attend(got, count) if size == owners else attend_ring(got, count)
    return unpack(exchange(result), count)


def members(owners):
    start = 5 * owners // 8
    return [(start + i) % owners for i in range(owners)]


def solution(mesh):
    spec = P(("batch", "slab"), None)
    return jax.shard_map(
        on_device, mesh=mesh, in_specs=(spec,) * 3, out_specs=spec, check_vma=False
    )
```

time: 45.7 us -> 41.7 us (0.912)
  blocking collectives: 38.8 us -> 34.3 us
  Pallas kernels: 3.87 us -> 4.33 us
    all_to_all x2, blocking collectives: 38.8 us -> 34.3 us  [exchange(): return lax.all_to_all(blocks, 'slab', 0, 0, axis_index_groups=groups)]
    pallas_call x1, Pallas kernels: 0.26 us -> 1.02 us  [pack(): pl.pallas_call(lambda *refs: pack_kernel(owners, *refs), out_shape=jax.Sh...]
where the time goes in v3:
time: 41.7 us; the launch traced here: 41.4 us
  blocking collectives  34.3 us (82%)
  Pallas kernels  4.33 us (10%)
  local copies, waits for them, and re-layouts  2.75 us (7%)
    all_to_all x2, blocking collectives, exchange(): return lax.all_to_all(blocks, 'slab', 0, 0, axis_index_groups=groups)  34.3 us
    unnamed x6, local copies, waits for them, and re-layouts  2.75 us
    pallas_call x1, Pallas kernels, attend(): pl.pallas_call(lambda *refs: attend_kernel(count, *refs), out_shape=jax.S...  2.48 us
    pallas_call x1, Pallas kernels, pack(): pl.pallas_call(lambda *refs: pack_kernel(owners, *refs), out_shape=jax.Sh...  1.02 us

profile of v3, /device:TPU:0, one launch (start us, length us, event | category | flops | bytes accessed | tf_op | source)
XLA Modules:
  0.0 41.4 jit_solution(12102468041290607808)
XLA Ops:
  0.0 0.0 copy-start
  0.0 0.9 %copy-done = bf16[56,1536]{1,0:T(8,128)(2,1)S(1)} copy-done((bf16[56,1536]{1,0:T(8,128)(2,1)S(1)}, bf16[56,1536]{1,0:T(8,128)(2,1)}, u32[]{:S(2)}) %copy-start) | copy-done | bytes 172056
  0.9 0.0 copy-start.1
  0.9 0.9 %copy-done.1 = bf16[56,1536]{1,0:T(8,128)(2,1)S(1)} copy-done((bf16[56,1536]{1,0:T(8,128)(2,1)S(1)}, bf16[56,1536]{1,0:T(8,128)(2,1)}, u32[]{:S(2)}) %copy-start.1) | copy-done | bytes 172056
  1.8 0.0 copy-start.2
  1.8 0.9 %copy-done.2 = bf16[56,1536]{1,0:T(8,128)(2,1)S(1)} copy-done((bf16[56,1536]{1,0:T(8,128)(2,1)S(1)}, bf16[56,1536]{1,0:T(8,128)(2,1)}, u32[]{:S(2)}) %copy-start.2) | copy-done | bytes 172056
  2.8 1.0 %shard_map.37 = bf16[16,160,128]{2,1,0:T(8,128)(2,1)S(1)} custom-call(bf16[56,1536]{1,0:T(8,128)(2,1)S(1)} %copy-done, bf16[56,1536]{1,0:T(8,128)(2,1)S(1)} %copy-done.1, bf16[56,1536]{1,0:T(8,128)(2,1)S(1)} %copy-done.2), custom_call_target="tpu_custom_call" | custom-call | tf_op jit(solution)/shard_map/pallas_call | solution.py:70
  3.8 24.2 %all_to_all.10.refs_0_ = bf16[16,160,128]{2,1,0:T(8,128)(2,1)S(1)} all-to-all(bf16[16,160,128]{2,1,0:T(8,128)(2,1)S(1)} %shard_map.37), channel_id=1, replica_groups={{20,22,24,26,28,30,0,2,4,6,8,10,12,14,16,18},{21,23,25,27,29,31,1,3,5,7..., dimensions={0} | all-to-all | bytes 1310720 | tf_op jit(solution)/shard_map/all_to_all | solution.py:199
  27.9 2.5 %shard_map.38 = bf16[16,48,128]{2,1,0:T(8,128)(2,1)S(1)} custom-call(bf16[16,160,128]{2,1,0:T(8,128)(2,1)S(1)} %all_to_all.10.refs_0_), custom_call_target="tpu_custom_call" | custom-call | tf_op jit(solution)/shard_map/pallas_call | solution.py:115
  30.4 10.2 %all_to_all.11.refs_0_ = bf16[16,48,128]{2,1,0:T(8,128)(2,1)S(1)} all-to-all(bf16[16,48,128]{2,1,0:T(8,128)(2,1)S(1)} %shard_map.38), channel_id=1, replica_groups={{20,22,24,26,28,30,0,2,4,6,8,10,12,14,16,18},{21,23,25,27,29,31,1,3,5,7..., dimensions={0} | all-to-all | bytes 393216 | tf_op jit(solution)/shard_map/all_to_all | solution.py:199
  40.6 0.8 %shard_map.39 = bf16[56,1536]{1,0:T(8,128)(2,1)} custom-call(bf16[16,48,128]{2,1,0:T(8,128)(2,1)S(1)} %all_to_all.11.refs_0_), custom_call_target="tpu_custom_call" | custom-call | tf_op jit(solution)/shard_map/pallas_call | solution.py:142
Async XLA Ops:
  0.0 0.9 %copy-start = (bf16[56,1536]{1,0:T(8,128)(2,1)S(1)}, bf16[56,1536]{1,0:T(8,128)(2,1)}, u32[]{:S(2)}) copy-start(bf16[56,1536]{1,0:T(8,128)(2,1)} %refs_0_.1) | copy-start | bytes 516100
  0.9 0.9 %copy-start.1 = (bf16[56,1536]{1,0:T(8,128)(2,1)S(1)}, bf16[56,1536]{1,0:T(8,128)(2,1)}, u32[]{:S(2)}) copy-start(bf16[56,1536]{1,0:T(8,128)(2,1)} %refs_1_.1) | copy-start | bytes 516100
  1.8 0.9 %copy-start.2 = (bf16[56,1536]{1,0:T(8,128)(2,1)S(1)}, bf16[56,1536]{1,0:T(8,128)(2,1)}, u32[]{:S(2)}) copy-start(bf16[56,1536]{1,0:T(8,128)(2,1)} %refs_2_.1) | copy-start | bytes 516100

commit v4 on v3

--- a/solution.py
+++ b/solution.py
@@ -65,7 +65,8 @@
                     out_ref[4 * m + i, 2 * count :] = fold(block, shared)
 
 
-def pack(owners, q, k, v):
+def pack(owners, *arrays):
+    q, k, v = (pltpu.with_memory_space_constraint(x, pltpu.HBM) for x in arrays)
     count = q.shape[0]
     return pl.pallas_call(
         lambda *refs: pack_kernel(owners, *refs),

time: 41.7 us -> 39.2 us (0.940)
  local copies, waits for them, and re-layouts: 2.75 us -> 0 us
    unnamed x6 -> x0, local copies, waits for them, and re-layouts: 2.75 us -> none
where the time goes in v4:
time: 39.2 us; the launch traced here: 39 us
  blocking collectives  34.3 us (87%)
  Pallas kernels  4.61 us (12%)
    all_to_all x2, blocking collectives, exchange(): return lax.all_to_all(blocks, 'slab', 0, 0, axis_index_groups=groups)  34.3 us
    pallas_call x1, Pallas kernels, attend(): pl.pallas_call(lambda *refs: attend_kernel(count, *refs), out_shape=jax.S...  2.48 us
    pallas_call x1, Pallas kernels, pack(): pl.pallas_call(lambda *refs: pack_kernel(owners, *refs), out_shape=jax.Sh...  1.31 us
    pallas_call x1, Pallas kernels, unpack(): pl.pallas_call(lambda *refs: unpack_kernel(count, *refs), out_shape=jax.S...  0.82 us

profile of v4, /device:TPU:0, one launch (start us, length us, event | category | flops | bytes accessed | tf_op | source)
XLA Modules:
  0.0 39.0 jit_solution(3203809077355499879)
XLA Ops:
  0.0 1.3 %shard_map.37 = bf16[16,160,128]{2,1,0:T(8,128)(2,1)S(1)} custom-call(bf16[56,1536]{1,0:T(8,128)(2,1)} %refs_0_.1, bf16[56,1536]{1,0:T(8,128)(2,1)} %refs_1_.1, bf16[56,1536]{1,0:T(8,128)(2,1)} %refs_2_.1), custom_call_target="tpu_custom_call" | custom-call | tf_op jit(solution)/shard_map/pallas_call | solution.py:71
  1.3 24.2 %all_to_all.10.refs_0_ = bf16[16,160,128]{2,1,0:T(8,128)(2,1)S(1)} all-to-all(bf16[16,160,128]{2,1,0:T(8,128)(2,1)S(1)} %shard_map.37), channel_id=1, replica_groups={{20,22,24,26,28,30,0,2,4,6,8,10,12,14,16,18},{21,23,25,27,29,31,1,3,5,7..., dimensions={0} | all-to-all | bytes 1310720 | tf_op jit(solution)/shard_map/all_to_all | solution.py:200
  25.5 2.5 %shard_map.38 = bf16[16,48,128]{2,1,0:T(8,128)(2,1)S(1)} custom-call(bf16[16,160,128]{2,1,0:T(8,128)(2,1)S(1)} %all_to_all.10.refs_0_), custom_call_target="tpu_custom_call" | custom-call | tf_op jit(solution)/shard_map/pallas_call | solution.py:116
  28.0 10.2 %all_to_all.11.refs_0_ = bf16[16,48,128]{2,1,0:T(8,128)(2,1)S(1)} all-to-all(bf16[16,48,128]{2,1,0:T(8,128)(2,1)S(1)} %shard_map.38), channel_id=1, replica_groups={{20,22,24,26,28,30,0,2,4,6,8,10,12,14,16,18},{21,23,25,27,29,31,1,3,5,7..., dimensions={0} | all-to-all | bytes 393216 | tf_op jit(solution)/shard_map/all_to_all | solution.py:200
  38.2 0.8 %shard_map.39 = bf16[56,1536]{1,0:T(8,128)(2,1)} custom-call(bf16[16,48,128]{2,1,0:T(8,128)(2,1)S(1)} %all_to_all.11.refs_0_), custom_call_target="tpu_custom_call" | custom-call | tf_op jit(solution)/shard_map/pallas_call | solution.py:143

commit v5 on v4

--- a/solution.py
+++ b/solution.py
@@ -94,17 +94,34 @@
         qc_ref[pl.ds(s * part, part), :] = jnp.where(first[:part], zero[:part], shared)
     factor = HEAD_DIM**-0.5 * LOG2E
 
-    def attended(q_ref, v_ref):
-        scores = lax.dot_general(
-            q_ref[...], k_ref[...], (((1,), (1,)), ((), ())), preferred_element_type=jnp.float32
-        )
+    def score(q_ref, rows):
+        return lax.dot_general(
+            q_ref[rows, :], k_ref[...], (((1,), (1,)), ((), ())), preferred_element_type=jnp.float32
+        )
+
+    def weigh(scores):
         top = jnp.max(scores, axis=-1, keepdims=True)
-        expo = jnp.exp2((scores - top) * factor).astype(k_ref.dtype)
-        mixed = jnp.dot(expo, v_ref[...], preferred_element_type=jnp.float32)
+        return jnp.exp2((scores - top) * factor).astype(k_ref.dtype)
+
+    def mix(weights, v_ref):
+        mixed = jnp.dot(weights, v_ref[...], preferred_element_type=jnp.float32)
         return (mixed / pltpu.roll(mixed, HEAD_DIM, 1)).astype(out_ref.dtype)
 
-    a = attended(qa_ref, va_ref)
-    c = attended(qc_ref, vc_ref)
+    half = owners // 2 * count
+    parts = (
+        (qa_ref, pl.ds(0, half), va_ref),
+        (qa_ref, pl.ds(half, half), va_ref),
+        (qc_ref, slice(None), vc_ref),
+    )
+    held, results = [], []
+    for step in range(len(parts) + 2):
+        if step < len(parts):
+            held.append(score(*parts[step][:2]))
+        if 1 <= step <= len(parts):
+            held[step - 1] = weigh(held[step - 1])
+        if step >= 2:
+            results.append(mix(held[step - 2], parts[step - 2][2]))
+    a, c = jnp.concatenate(results[:2], axis=0), results[2]
     for s in range(owners):
         out_ref[s] = fold(a[s * count : (s + 1) * count], c[s * part : (s + 1) * part])
 

time: 39.2 us -> 38.6 us (0.985)
  Pallas kernels: 4.61 us -> 4.01 us
    pallas_call x1, Pallas kernels: 2.48 us -> 1.88 us  [attend(): pl.pallas_call(lambda *refs: attend_kernel(count, *refs), out_shape=jax.S...]
where the time goes in v5:
time: 38.6 us; the launch traced here: 38.4 us
  blocking collectives  34.3 us (89%)
  Pallas kernels  4.01 us (10%)
    all_to_all x2, blocking collectives, exchange(): return lax.all_to_all(blocks, 'slab', 0, 0, axis_index_groups=groups)  34.3 us
    pallas_call x1, Pallas kernels, attend(): pl.pallas_call(lambda *refs: attend_kernel(count, *refs), out_shape=jax.S...  1.88 us
    pallas_call x1, Pallas kernels, pack(): pl.pallas_call(lambda *refs: pack_kernel(owners, *refs), out_shape=jax.Sh...  1.31 us
    pallas_call x1, Pallas kernels, unpack(): pl.pallas_call(lambda *refs: unpack_kernel(count, *refs), out_shape=jax.S...  0.82 us

profile of v5, /device:TPU:0, one launch (start us, length us, event | category | flops | bytes accessed | tf_op | source)
XLA Modules:
  0.0 38.4 jit_solution(11239359284152947864)
XLA Ops:
  0.0 1.3 %shard_map.37 = bf16[16,160,128]{2,1,0:T(8,128)(2,1)S(1)} custom-call(bf16[56,1536]{1,0:T(8,128)(2,1)} %refs_0_.1, bf16[56,1536]{1,0:T(8,128)(2,1)} %refs_1_.1, bf16[56,1536]{1,0:T(8,128)(2,1)} %refs_2_.1), custom_call_target="tpu_custom_call" | custom-call | tf_op jit(solution)/shard_map/pallas_call | solution.py:71
  1.3 24.2 %all_to_all.10.refs_0_ = bf16[16,160,128]{2,1,0:T(8,128)(2,1)S(1)} all-to-all(bf16[16,160,128]{2,1,0:T(8,128)(2,1)S(1)} %shard_map.37), channel_id=1, replica_groups={{20,22,24,26,28,30,0,2,4,6,8,10,12,14,16,18},{21,23,25,27,29,31,1,3,5,7..., dimensions={0} | all-to-all | bytes 1310720 | tf_op jit(solution)/shard_map/all_to_all | solution.py:217
  25.5 1.9 %shard_map.38 = bf16[16,48,128]{2,1,0:T(8,128)(2,1)S(1)} custom-call(bf16[16,160,128]{2,1,0:T(8,128)(2,1)S(1)} %all_to_all.10.refs_0_), custom_call_target="tpu_custom_call" | custom-call | tf_op jit(solution)/shard_map/pallas_call | solution.py:133
  27.4 10.2 %all_to_all.11.refs_0_ = bf16[16,48,128]{2,1,0:T(8,128)(2,1)S(1)} all-to-all(bf16[16,48,128]{2,1,0:T(8,128)(2,1)S(1)} %shard_map.38), channel_id=1, replica_groups={{20,22,24,26,28,30,0,2,4,6,8,10,12,14,16,18},{21,23,25,27,29,31,1,3,5,7..., dimensions={0} | all-to-all | bytes 393216 | tf_op jit(solution)/shard_map/all_to_all | solution.py:217
  37.6 0.8 %shard_map.39 = bf16[56,1536]{1,0:T(8,128)(2,1)} custom-call(bf16[16,48,128]{2,1,0:T(8,128)(2,1)S(1)} %all_to_all.11.refs_0_), custom_call_target="tpu_custom_call" | custom-call | tf_op jit(solution)/shard_map/pallas_call | solution.py:160

commit v6 on v5

--- a/solution.py
+++ b/solution.py
@@ -222,8 +222,8 @@
 
 
 def members(owners):
-    start = 5 * owners // 8
-    return [(start + i) % owners for i in range(owners)]
+    middle = 5 * owners // 8
+    return [middle] + [i ^ 1 for i in range(owners) if i ^ 1 != middle]
 
 
 def solution(mesh):

time: 38.6 us -> 37.9 us (0.982)
  blocking collectives: 34.3 us -> 33.6 us
    all_to_all x2, blocking collectives: 34.3 us -> 33.6 us  [exchange(): return lax.all_to_all(blocks, 'slab', 0, 0, axis_index_groups=groups)]
where the time goes in v6:
time: 37.9 us; the launch traced here: 37.7 us
  blocking collectives  33.6 us (89%)
  Pallas kernels  4.01 us (11%)
    all_to_all x2, blocking collectives, exchange(): return lax.all_to_all(blocks, 'slab', 0, 0, axis_index_groups=groups)  33.6 us
    pallas_call x1, Pallas kernels, attend(): pl.pallas_call(lambda *refs: attend_kernel(count, *refs), out_shape=jax.S...  1.88 us
    pallas_call x1, Pallas kernels, pack(): pl.pallas_call(lambda *refs: pack_kernel(owners, *refs), out_shape=jax.Sh...  1.31 us
    pallas_call x1, Pallas kernels, unpack(): pl.pallas_call(lambda *refs: unpack_kernel(count, *refs), out_shape=jax.S...  0.82 us

profile of v6, /device:TPU:0, one launch (start us, length us, event | category | flops | bytes accessed | tf_op | source)
XLA Modules:
  0.0 37.7 jit_solution(7320972927850181401)
XLA Ops:
  0.0 1.3 %shard_map.37 = bf16[16,160,128]{2,1,0:T(8,128)(2,1)S(1)} custom-call(bf16[56,1536]{1,0:T(8,128)(2,1)} %refs_0_.1, bf16[56,1536]{1,0:T(8,128)(2,1)} %refs_1_.1, bf16[56,1536]{1,0:T(8,128)(2,1)} %refs_2_.1), custom_call_target="tpu_custom_call" | custom-call | tf_op jit(solution)/shard_map/pallas_call | solution.py:71
  1.3 24.2 %all_to_all.10.refs_0_ = bf16[16,160,128]{2,1,0:T(8,128)(2,1)S(1)} all-to-all(bf16[16,160,128]{2,1,0:T(8,128)(2,1)S(1)} %shard_map.37), channel_id=1, replica_groups={{20,2,0,6,4,10,8,14,12,18,16,22,26,24,30,28},{21,3,1,7,5,11,9,15,13,19,..., dimensions={0} | all-to-all | bytes 1310720 | tf_op jit(solution)/shard_map/all_to_all | solution.py:217
  25.6 1.9 %shard_map.38 = bf16[16,48,128]{2,1,0:T(8,128)(2,1)S(1)} custom-call(bf16[16,160,128]{2,1,0:T(8,128)(2,1)S(1)} %all_to_all.10.refs_0_), custom_call_target="tpu_custom_call" | custom-call | tf_op jit(solution)/shard_map/pallas_call | solution.py:133
  27.5 9.4 %all_to_all.11.refs_0_ = bf16[16,48,128]{2,1,0:T(8,128)(2,1)S(1)} all-to-all(bf16[16,48,128]{2,1,0:T(8,128)(2,1)S(1)} %shard_map.38), channel_id=1, replica_groups={{20,2,0,6,4,10,8,14,12,18,16,22,26,24,30,28},{21,3,1,7,5,11,9,15,13,19,..., dimensions={0} | all-to-all | bytes 393216 | tf_op jit(solution)/shard_map/all_to_all | solution.py:217
  36.8 0.8 %shard_map.39 = bf16[56,1536]{1,0:T(8,128)(2,1)} custom-call(bf16[16,48,128]{2,1,0:T(8,128)(2,1)S(1)} %all_to_all.11.refs_0_), custom_call_target="tpu_custom_call" | custom-call | tf_op jit(solution)/shard_map/pallas_call | solution.py:160

commit v7 on v6

--- a/solution.py
+++ b/solution.py
@@ -222,8 +222,8 @@
 
 
 def members(owners):
-    middle = 5 * owners // 8
-    return [middle] + [i ^ 1 for i in range(owners) if i ^ 1 != middle]
+    order = (11, 8, 3, 15, 10, 7, 2, 0, 4, 14, 5, 1, 9, 13, 6, 12)
+    return list(order) if len(order) == owners else list(range(owners))
 
 
 def solution(mesh):

time: 37.9 us -> 37.3 us (0.984)
  blocking collectives: 33.6 us -> 33.1 us
    all_to_all x2, blocking collectives: 33.6 us -> 33.1 us  [exchange(): return lax.all_to_all(blocks, 'slab', 0, 0, axis_index_groups=groups)]
where the time goes in v7:
time: 37.3 us; the launch traced here: 37.1 us
  blocking collectives  33.1 us (89%)
  Pallas kernels  4.01 us (11%)
    all_to_all x2, blocking collectives, exchange(): return lax.all_to_all(blocks, 'slab', 0, 0, axis_index_groups=groups)  33.1 us
    pallas_call x1, Pallas kernels, attend(): pl.pallas_call(lambda *refs: attend_kernel(count, *refs), out_shape=jax.S...  1.88 us
    pallas_call x1, Pallas kernels, pack(): pl.pallas_call(lambda *refs: pack_kernel(owners, *refs), out_shape=jax.Sh...  1.31 us
    pallas_call x1, Pallas kernels, unpack(): pl.pallas_call(lambda *refs: unpack_kernel(count, *refs), out_shape=jax.S...  0.82 us

profile of v7, /device:TPU:0, one launch (start us, length us, event | category | flops | bytes accessed | tf_op | source)
XLA Modules:
  0.0 37.1 jit_solution(13100223165904772062)
XLA Ops:
  0.0 1.3 %shard_map.37 = bf16[16,160,128]{2,1,0:T(8,128)(2,1)S(1)} custom-call(bf16[56,1536]{1,0:T(8,128)(2,1)} %refs_0_.1, bf16[56,1536]{1,0:T(8,128)(2,1)} %refs_1_.1, bf16[56,1536]{1,0:T(8,128)(2,1)} %refs_2_.1), custom_call_target="tpu_custom_call" | custom-call | tf_op jit(solution)/shard_map/pallas_call | solution.py:71
  1.3 23.4 %all_to_all.10.refs_0_ = bf16[16,160,128]{2,1,0:T(8,128)(2,1)S(1)} all-to-all(bf16[16,160,128]{2,1,0:T(8,128)(2,1)S(1)} %shard_map.37), channel_id=1, replica_groups={{22,16,6,30,20,14,4,0,8,28,10,2,18,26,12,24},{23,17,7,31,21,15,5,1,9,29..., dimensions={0} | all-to-all | bytes 1310720 | tf_op jit(solution)/shard_map/all_to_all | solution.py:217
  24.8 1.9 %shard_map.38 = bf16[16,48,128]{2,1,0:T(8,128)(2,1)S(1)} custom-call(bf16[16,160,128]{2,1,0:T(8,128)(2,1)S(1)} %all_to_all.10.refs_0_), custom_call_target="tpu_custom_call" | custom-call | tf_op jit(solution)/shard_map/pallas_call | solution.py:133
  26.6 9.7 %all_to_all.11.refs_0_ = bf16[16,48,128]{2,1,0:T(8,128)(2,1)S(1)} all-to-all(bf16[16,48,128]{2,1,0:T(8,128)(2,1)S(1)} %shard_map.38), channel_id=1, replica_groups={{22,16,6,30,20,14,4,0,8,28,10,2,18,26,12,24},{23,17,7,31,21,15,5,1,9,29..., dimensions={0} | all-to-all | bytes 393216 | tf_op jit(solution)/shard_map/all_to_all | solution.py:217
  36.3 0.8 %shard_map.39 = bf16[56,1536]{1,0:T(8,128)(2,1)} custom-call(bf16[16,48,128]{2,1,0:T(8,128)(2,1)S(1)} %all_to_all.11.refs_0_), custom_call_target="tpu_custom_call" | custom-call | tf_op jit(solution)/shard_map/pallas_call | solution.py:160
